TPU v7x, 32 devices: a whole 2x2x4 slice. The times are simulated.
32 devices in a mesh: strip: 4 (over y, core), wide: 4 (over z), comp: 2 (over x).
Axes of the slice: x: 2, y: 2, z: 4, core: 2. Of those that a mesh axis runs over, the one named last changes fastest.
Arguments:
- spectrum: bfloat16 [1152, 49152], P('comp', ('strip', 'wide')), may hold values from 0.049804688 to 2
- wet_mask: int32 [192, 256], P('strip'), may hold values 0 or 1
- currents: float32 [2, 32, 16], P(None, 'strip', 'wide'), may hold values from -3 to 3
- remap_index: int32 [4, 49152], P(None, 'strip'), may hold values from 0 to 127, as said below
- remap_weights: float32 [4, 49152], P(None, 'strip'), may hold values from 0.2 to 0.6
- source_matrix: bfloat16 [1152, 1152], P('comp'), may hold values from -0.1875 to 0.1875
Outputs:
- updated: bfloat16 [1152, 49152], P('comp', ('strip', 'wide'))
- stokes: float32 [2, 32, 49152], P(None, 'comp', ('strip', 'wide'))
Inputs may be any that keep to these rules, and one draw needn't show every extreme that they name: `remap_index`: a point's cells lie in the ocean rows and columns of its strip next to the point's own location.
All inputs are finite; a program needn't handle non-finite values. No bound on the sum of `wet_mask` on one device may be relied on, other than what follows from the above.
Results may differ from a plain program's by a relative error of at most 0.0048.
Values may be sent and summed in bfloat16 or wider, within the bound.
A program may use at most 128 MiB of HBM per device.

v0:
```python
import math

import jax
import jax.numpy as jnp
from jax import lax
from jax.sharding import PartitionSpec as P

NFREQ = 32
NDIR = 36
LEVELS = 32
SUBSTEPS = 4


courant = 0.45


def extended(cells, sides, width):
    for axis, dim in sides:
        count = lax.axis_size(axis)
        ends = count - 1
        head = lax.slice_in_dim(cells, 0, width, axis=dim)
        tail = lax.slice_in_dim(cells, cells.shape[dim] - width, cells.shape[dim], axis=dim)
        cells = jnp.concatenate(
            [
                lax.ppermute(tail, axis, [(i, (i + 1) % count) for i in range(ends)]),
                cells,
                lax.ppermute(head, axis, [((i + 1) % count, i) for i in range(ends)]),
            ],
            axis=dim,
        )
    return cells


def bin_speeds(first_bin, bin_count):
    index = first_bin + jnp.arange(bin_count, dtype=jnp.int32)
    freq_index = (index // NDIR).astype(jnp.float32)
    dir_index = (index % NDIR).astype(jnp.float32)
    group_speed = 0.35 + 0.65 * (NFREQ - 1 - freq_index) / (NFREQ - 1)
    heading = 2.0 * math.pi * (dir_index + 0.5) / NDIR
    return (
        (group_speed * jnp.cos(heading))[:, None, None],
        (group_speed * jnp.sin(heading))[:, None, None],
    )


def stokes_kernel(bin_count, first_level, level_count):
    index = jnp.arange(bin_count, dtype=jnp.int32)
    frequency = (index // NDIR + 1).astype(jnp.float32)
    heading = 2.0 * math.pi * ((index % NDIR).astype(jnp.float32) + 0.5) / NDIR
    level_index = (first_level + jnp.arange(level_count, dtype=jnp.int32)).astype(jnp.float32)
    damping = jnp.exp(-4.0 * frequency[None, :] * (level_index[:, None] + 0.5) / (NFREQ * LEVELS))
    amplitude = damping * (frequency / NFREQ)[None, :] / math.sqrt(NDIR)
    eastward = amplitude * jnp.cos(heading)[None, :]
    northward = amplitude * jnp.sin(heading)[None, :]
    return jnp.concatenate([eastward, northward], 0).astype(jnp.bfloat16)


def substep(energy, east_flow, north_flow, wet_frac, speed_east, speed_north):
    east_speed = speed_east + east_flow[None]
    north_speed = speed_north + north_flow[None]
    flux_lon = jnp.maximum(east_speed, 0.0) * energy + jnp.minimum(
        jnp.roll(east_speed, -1, 2), 0.0
    ) * jnp.roll(energy, -1, 2)
    flux_lat = (
        jnp.maximum(north_speed[:, :-1], 0.0) * energy[:, :-1]
        + jnp.minimum(north_speed[:, 1:], 0.0) * energy[:, 1:]
    )
    spread = flux_lon - jnp.roll(flux_lon, 1, 2)
    change = spread[:, 1:-1] + flux_lat[:, 1:] - flux_lat[:, :-1]
    return wet_frac[1:-1] * (energy[:, 1:-1] - courant * change)


def advance(widened, speed_east, speed_north):
    bin_share = speed_east.shape[0]
    energy = widened[:bin_share]
    east_flow = widened[bin_share]
    north_flow = widened[bin_share + 1]
    wet_frac = widened[bin_share + 2]
    energy = substep(energy, east_flow, north_flow, wet_frac, speed_east, speed_north)
    return energy


def interpolate(tiles, remap_index, remap_weights, lat_rows, lon_cells):
    ocean_rows = tiles.shape[1]
    ocean_cols = tiles.shape[2]
    block_points = 4 * lon_cells
    block_count = lat_rows // 4
    flow_table = tiles.reshape(2 * ocean_rows, ocean_cols)
    index_blocks = jnp.transpose(remap_index.reshape(4, block_count, block_points), (1, 0, 2))
    weight_blocks = jnp.transpose(remap_weights.reshape(4, block_count, block_points), (1, 0, 2))
    column_ids = jnp.arange(ocean_cols, dtype=jnp.int32)[None, :, None]
    row_ids = jnp.arange(ocean_rows, dtype=jnp.int32)[None, :, None]

    def one_block(inputs):
        cells, shares = inputs
        column_of = cells % ocean_cols
        row_of = cells // ocean_cols
        column_hot = (column_of[:, None, :] == column_ids).astype(jnp.float32)
        picked = jnp.einsum("mk,jkp->jmp", flow_table, column_hot, precision=lax.Precision.HIGHEST)
        picked = picked.reshape(4, 2, ocean_rows, block_points)
        row_weight = (row_of[:, None, :] == row_ids).astype(jnp.float32) * shares[:, None, :]
        return jnp.sum(picked * row_weight[:, None], (0, 2))

    blocks = lax.map(one_block, (index_blocks, weight_blocks))
    return jnp.transpose(blocks, (1, 0, 2)).reshape(2, lat_rows, lon_cells)


def per_device(spectrum, wet_mask, currents, remap_index, remap_weights, source_matrix):
    wide_count = lax.axis_size("wide")
    wide_index = lax.axis_index("wide")
    comp_index = lax.axis_index("comp")
    lat_rows, lon_cells = wet_mask.shape
    local_bins, points = spectrum.shape
    tiles = lax.all_gather(currents, "wide", axis=2, tiled=True)
    surface = interpolate(tiles, remap_index, remap_weights, lat_rows, lon_cells)
    wet_frac = wet_mask.astype(jnp.float32)
    row_count = lat_rows // wide_count
    wet_rows = lax.dynamic_slice_in_dim(wet_frac, wide_index * row_count, row_count, 0)
    flow_rows = lax.dynamic_slice_in_dim(surface, wide_index * row_count, row_count, 1)
    speed_east, speed_north = bin_speeds(comp_index * local_bins, local_bins)
    energy = spectrum.astype(jnp.float32).reshape(local_bins, row_count, lon_cells) * wet_rows
    for repeat in range(SUBSTEPS):
        fields = jnp.concatenate([energy, flow_rows, wet_rows[None]], 0)
        widened = extended(fields, ((("strip", "wide"), 1),), 1)
        energy = advance(widened, speed_east, speed_north)
    returned = energy.astype(jnp.bfloat16).reshape(local_bins, points)
    level_rows = LEVELS // lax.axis_size("comp")
    first_level = comp_index * level_rows
    fragment = lax.all_gather(returned, "comp", axis=0, tiled=True)
    width = fragment.shape[0]
    kernel = stokes_kernel(width, first_level, level_rows)
    source_part = jnp.dot(source_matrix, fragment, preferred_element_type=jnp.float32)
    drift_part = jnp.dot(kernel, fragment, preferred_element_type=jnp.float32)
    wet_points = lax.dynamic_slice_in_dim(wet_frac.reshape(-1), wide_index * points, points, 0)
    updated = (
        wet_points[None, :] * jnp.maximum(returned.astype(jnp.float32) + source_part, 0.0)
    ).astype(jnp.bfloat16)
    return (updated, drift_part.reshape(2, level_rows, points))


def solution(mesh):
    placed = (
        P("comp", ("strip", "wide")),
        P("strip", None),
        P(None, "strip", "wide"),
        P(None, "strip"),
        P(None, "strip"),
        P("comp", None),
    )
    return jax.shard_map(
        per_device,
        mesh=mesh,
        in_specs=placed,
        out_specs=(P("comp", ("strip", "wide")), P(None, "comp", ("strip", "wide"))),
        check_vma=False,
    )
```

profile of v0, /device:TPU:1, one launch (start us, length us, event | category | flops | bytes accessed | tf_op | source)
XLA Modules:
  0.0 619.4 jit_solution(8049123147209325)
XLA Ops:
  10.0 11.3 %all_gather.6 = f32[2,8,16]{1,0,2:T(2,128)S(1)} all-gather(f32[2,8,4]{1,0,2:T(2,128)S(1)} %copy.94), channel_id=1, replica_groups=mesh['strip'=4,'wide'=4,'comp'=2] {'wide'}, dimensions={2}, use_global_device_ids=true | all-gather | bytes 1280 | tf_op jit(solution)/shard_map/all_gather | solution.py:114
  21.3 30.7 %while.13 = (s32[]{:T(128)}, f32[12,2,1024]{2,1,0:T(2,128)S(1)}, s32[12,4,1024]{2,1,0:T(4,128)}, f32[16,16]{1,0:T(8,128)S(1)}, f32[12,4,1024]{2,1,0:T(4,128)}, /*index=5*/s32[]{:T(128)}) while((s32[]{:T(128)}, f32[12,2,1024]{2,1,0:T(2,128)S(1)}, s32[12,4,1024]{2,1,0:T(4,128)}, f32[16,16]{1,0:T(8,128)S(1)}, ...), condition=%wide.region_3.4_spmd.clone, body=%wide.region_0.3_spmd.clone.sunk | while | flops 12945410 | bytes 574557 | solution.py:104
  52.1 4.0 copy.128
  56.1 2.7 constant_dynamic-slice_fusion
  58.7 6.3 %copy.93 = f32[576,3072]{0,1:T(8,128)} copy(bf16[576,3072]{1,0:T(8,128)(2,1)} %param.8) | data formatting | bytes 10616832 | tf_op jit(solution)/shard_map/reshape | solution.py:121
  65.1 3.9 broadcast_multiply_fusion
  69.0 2.6 pad_maximum_fusion.27
  73.0 2.1 copy.100
  75.0 8.4 %collective-permute-start.1 = (f32[579,1,256]{2,1,0:T(1,128)}, f32[579,1,256]{2,1,0:T(1,128)}, u32[]{:S(2)}, u32[]{:S(2)}) collective-permute-start(f32[579,1,256]{2,1,0:T(1,128)} %copy.100), channel_id=1, source_target_pairs={{2,0},{4,2},{6,4},{8,6},{10,8},{12,10},{14,12},{16,14},{18,16},{20... | collective-permute-start | bytes 1778696 | tf_op jit(solution)/shard_map/ppermute | solution.py:27
  84.6 2.1 collective-permute-start
  88.0 6.8 %collective-permute-done.1 = f32[579,1,256]{2,1,0:T(1,128)} collective-permute-done((f32[579,1,256]{2,1,0:T(1,128)}, f32[579,1,256]{2,1,0:T(1,128)}, u32[]{:S(2)}, u32[]{:S(2)}) %collective-permute-start.1) | collective-permute-done | bytes 592928 | tf_op jit(solution)/shard_map/ppermute | solution.py:27
  96.1 10.6 %collective-permute-done = f32[579,1,256]{2,1,0:T(1,128)} collective-permute-done((f32[579,1,256]{2,1,0:T(1,128)}, f32[579,1,256]{2,1,0:T(1,128)}, u32[]{:S(2)}, u32[]{:S(2)}) %collective-permute-start) | collective-permute-done | bytes 592928 | tf_op jit(solution)/shard_map/ppermute | solution.py:25
  108.7 5.3 fusion.12
  116.0 4.3 broadcast_add_fusion.6
  120.4 4.4 slice.352
  125.9 8.2 %slice.354 = f32[576,14,255]{0,2,1:T(8,128)} slice(f32[579,14,256]{0,2,1:T(8,128)} %copy-done.11), slice={[0:576], [0:14], [1:256]} | slice | bytes 16450560 | tf_op jit(solution)/shard_map/jit(_roll_static)/slice | solution.py:63
  134.2 11.4 %fusion.29 = f32[576,13,256]{0,2,1:T(8,128)} fusion(f32[1,12,256]{0,2,1:T(8,128)S(1)} %copy.98, f32[2,12,256]{0,2,1:T(8,128)S(1)} %copy-done.2, f32[579,1,256]{0,2,1:T(8,128)S(1)} %copy.102, f32[576,12,256]{0,2,1:T(8,128)S(1)} %bitcast.89, f32[576,14,256]{0,2,1:T(8,128)} %get-tuple-element.145, f32[579,1,256]{0,2,1:T(8,128)S(1)} %copy-done.19), kind=kLoop, calls=%fused_computation.81 | loop fusion | flops 21086208 | bytes 31303680 | tf_op jit(solution)/shard_map/add | solution.py:65
  145.6 12.0 %fusion.22 = f32[576,14,256]{0,2,1:T(8,128)S(1)} fusion(f32[579,14,256]{0,2,1:T(8,128)} %copy-done.11, f32[576,14,1]{0,2,1:T(1,128)S(1)} %slice.353, f32[576,14,255]{0,2,1:T(8,128)} %slice.352, f32[576,14,1]{0,2,1:T(1,128)S(1)} %slice.355, f32[576,14,255]{0,2,1:T(8,128)} %slice.354, f32[14,256]{1,0:T(8,128)S(1)} %get-tuple-element.119, f32[576]{0:T(1024)S(1)} %copy-done.28), kind=kLoop, calls=%fused_computation.70 | loop fusion | flops 16515072 | bytes 33046784 | tf_op jit(solution)/shard_map/add | solution.py:61
  157.7 3.5 copy-done.14
  161.2 13.7 %fusion.59 = f32[576,12,256]{0,2,1:T(8,128)S(1)} fusion(f32[576,13,256]{0,2,1:T(8,128)} %fusion.29, f32[576,14,256]{0,2,1:T(8,128)} %copy-done.14, f32[576,14,255]{0,2,1:T(8,128)} %bitcast.93, f32[576,14,1]{0,2,1:T(1,128)S(1)} %slice.356, f32[12,256]{1,0:T(8,128)S(1)} %copy-done.24, f32[576,12,256]{0,2,1:T(8,128)} %bitcast.97), kind=kLoop, calls=%fused_computation.132 | loop fusion | flops 14155776 | bytes 43659264 | tf_op jit(solution)/shard_map/mul | solution.py:70
  175.0 2.6 pad_maximum_fusion.26
  179.0 2.1 copy.107
  181.0 2.3 collective-permute-start.3
  184.5 3.3 collective-permute-start.2
  187.8 8.8 %collective-permute-done.3 = f32[579,1,256]{2,1,0:T(1,128)} collective-permute-done((f32[579,1,256]{2,1,0:T(1,128)}, f32[579,1,256]{2,1,0:T(1,128)}, u32[]{:S(2)}, u32[]{:S(2)}) %collective-permute-start.3) | collective-permute-done | bytes 592928 | tf_op jit(solution)/shard_map/ppermute | solution.py:27
  198.0 9.0 %collective-permute-done.2 = f32[579,1,256]{2,1,0:T(1,128)} collective-permute-done((f32[579,1,256]{2,1,0:T(1,128)}, f32[579,1,256]{2,1,0:T(1,128)}, u32[]{:S(2)}, u32[]{:S(2)}) %collective-permute-start.2) | collective-permute-done | bytes 592928 | tf_op jit(solution)/shard_map/ppermute | solution.py:25
  209.0 5.3 fusion.14
  216.9 3.9 copy-done.15
  220.9 8.1 %slice.368 = f32[576,14,255]{0,2,1:T(8,128)} slice(f32[576,14,256]{0,2,1:T(8,128)} %copy-done.15), slice={[0:576], [0:14], [1:256]} | slice | bytes 16450560 | tf_op jit(solution)/shard_map/jit(_roll_static)/slice | solution.py:62
  229.1 8.2 %slice.370 = f32[576,14,255]{0,2,1:T(8,128)} slice(f32[579,14,256]{0,2,1:T(8,128)} %copy-done.12), slice={[0:576], [0:14], [1:256]} | slice | bytes 16450560 | tf_op jit(solution)/shard_map/jit(_roll_static)/slice | solution.py:63
  237.3 4.2 broadcast_add_fusion.4
  241.5 11.5 %fusion.32 = f32[576,13,256]{0,2,1:T(8,128)} fusion(f32[1,12,256]{0,2,1:T(8,128)S(1)} %copy.98, f32[2,12,256]{0,2,1:T(8,128)S(1)} %copy-done.3, f32[579,1,256]{0,2,1:T(8,128)S(1)} %copy.109, f32[576,12,256]{0,2,1:T(8,128)S(1)} %bitcast.85, f32[576,14,256]{0,2,1:T(8,128)} %broadcast_add_fusion.4, f32[579,1,256]{0,2,1:T(8,128)S(1)} %copy-done.21), kind=kLoop, calls=%fused_computation.84 | loop fusion | flops 21086208 | bytes 31303680 | tf_op jit(solution)/shard_map/add | solution.py:65
  253.0 15.9 %fusion.21 = f32[576,14,256]{0,2,1:T(8,128)} fusion(f32[579,14,256]{0,2,1:T(8,128)} %copy-done.12, f32[576,14,1]{0,2,1:T(1,128)S(1)} %slice.369, f32[576,14,255]{0,2,1:T(8,128)} %slice.368, f32[576,14,1]{0,2,1:T(1,128)S(1)} %slice.371, f32[576,14,255]{0,2,1:T(8,128)} %slice.370, f32[14,256]{1,0:T(8,128)S(1)} %get-tuple-element.117, f32[576]{0:T(1024)S(1)} %copy-done.29), kind=kLoop, calls=%fused_computation.68 | loop fusion | flops 16515072 | bytes 33046784 | tf_op jit(solution)/shard_map/add | solution.py:61
  269.9 13.3 %fusion.56 = f32[576,12,256]{0,2,1:T(8,128)S(1)} fusion(f32[576,12,256]{0,2,1:T(8,128)S(1)} %bitcast.85, f32[576,13,256]{0,2,1:T(8,128)} %fusion.32, f32[576,14,256]{0,2,1:T(8,128)} %fusion.21, f32[576,14,255]{0,2,1:T(8,128)} %bitcast.94, f32[576,14,1]{0,2,1:T(1,128)S(1)} %slice.372, f32[12,256]{1,0:T(8,128)S(1)} %copy-done.25), kind=kLoop, calls=%fused_computation.125 | loop fusion | flops 12386304 | bytes 43659264 | tf_op jit(solution)/shard_map/mul | solution.py:70
  283.2 2.8 pad_maximum_fusion.25
  287.2 2.1 copy.114
  289.3 2.8 collective-permute-start.5
  293.2 4.1 collective-permute-start.4
  297.3 23.0 %collective-permute-done.5 = f32[579,1,256]{2,1,0:T(1,128)} collective-permute-done((f32[579,1,256]{2,1,0:T(1,128)}, f32[579,1,256]{2,1,0:T(1,128)}, u32[]{:S(2)}, u32[]{:S(2)}) %collective-permute-start.5) | collective-permute-done | bytes 592928 | tf_op jit(solution)/shard_map/ppermute | solution.py:27
  323.7 5.3 fusion.16
  332.5 3.6 copy-done.16
  336.2 8.1 %slice.384 = f32[576,14,255]{0,2,1:T(8,128)} slice(f32[576,14,256]{0,2,1:T(8,128)} %copy-done.16), slice={[0:576], [0:14], [1:256]} | slice | bytes 16450560 | tf_op jit(solution)/shard_map/jit(_roll_static)/slice | solution.py:62
  345.3 8.2 %slice.386 = f32[576,14,255]{0,2,1:T(8,128)} slice(f32[579,14,256]{0,2,1:T(8,128)} %copy-done.13), slice={[0:576], [0:14], [1:256]} | slice | bytes 16450560 | tf_op jit(solution)/shard_map/jit(_roll_static)/slice | solution.py:63
  353.6 4.2 broadcast_add_fusion.2
  357.8 11.5 %fusion.35 = f32[576,13,256]{0,2,1:T(8,128)} fusion(f32[1,12,256]{0,2,1:T(8,128)S(1)} %copy.98, f32[2,12,256]{0,2,1:T(8,128)S(1)} %copy-done.4, f32[579,1,256]{0,2,1:T(8,128)S(1)} %copy.116, f32[576,12,256]{0,2,1:T(8,128)S(1)} %bitcast.87, f32[576,14,256]{0,2,1:T(8,128)} %broadcast_add_fusion.2, f32[579,1,256]{0,2,1:T(8,128)S(1)} %copy-done.22), kind=kLoop, calls=%fused_computation.87 | loop fusion | flops 21086208 | bytes 31303680 | tf_op jit(solution)/shard_map/add | solution.py:65
  369.3 15.9 %fusion.20 = f32[576,14,256]{0,2,1:T(8,128)} fusion(f32[579,14,256]{0,2,1:T(8,128)} %copy-done.13, f32[576,14,1]{0,2,1:T(1,128)S(1)} %slice.385, f32[576,14,255]{0,2,1:T(8,128)} %slice.384, f32[576,14,1]{0,2,1:T(1,128)S(1)} %slice.387, f32[576,14,255]{0,2,1:T(8,128)} %slice.386, f32[14,256]{1,0:T(8,128)S(1)} %get-tuple-element.115, f32[576]{0:T(1024)S(1)} %copy-done.30), kind=kLoop, calls=%fused_computation.66 | loop fusion | flops 16515072 | bytes 33046784 | tf_op jit(solution)/shard_map/add | solution.py:61
  386.2 13.2 %fusion.53 = f32[576,12,256]{0,2,1:T(8,128)S(1)} fusion(f32[576,12,256]{0,2,1:T(8,128)S(1)} %bitcast.87, f32[576,13,256]{0,2,1:T(8,128)} %fusion.35, f32[576,14,256]{0,2,1:T(8,128)} %fusion.20, f32[576,14,255]{0,2,1:T(8,128)} %bitcast.95, f32[576,14,1]{0,2,1:T(1,128)S(1)} %slice.388, f32[12,256]{1,0:T(8,128)S(1)} %copy-done.26), kind=kLoop, calls=%fused_computation.118 | loop fusion | flops 12386304 | bytes 43659264 | tf_op jit(solution)/shard_map/mul | solution.py:70
  399.5 2.8 pad_maximum_fusion.24
  403.5 2.1 copy.121
  408.6 3.7 collective-permute-start.6
  412.3 10.7 %collective-permute-done.7 = f32[579,1,256]{2,1,0:T(1,128)} collective-permute-done((f32[579,1,256]{2,1,0:T(1,128)}, f32[579,1,256]{2,1,0:T(1,128)}, u32[]{:S(2)}, u32[]{:S(2)}) %collective-permute-start.7) | collective-permute-done | bytes 592928 | tf_op jit(solution)/shard_map/ppermute | solution.py:27
  424.2 12.1 %collective-permute-done.6 = f32[579,1,256]{2,1,0:T(1,128)} collective-permute-done((f32[579,1,256]{2,1,0:T(1,128)}, f32[579,1,256]{2,1,0:T(1,128)}, u32[]{:S(2)}, u32[]{:S(2)}) %collective-permute-start.6) | collective-permute-done | bytes 592928 | tf_op jit(solution)/shard_map/ppermute | solution.py:25
  438.4 5.3 fusion.18
  446.4 3.7 copy-done.17
  450.7 8.2 %slice.400 = f32[576,14,255]{0,2,1:T(8,128)} slice(f32[576,14,256]{0,2,1:T(8,128)} %copy-done.17), slice={[0:576], [0:14], [1:256]} | slice | bytes 16450560 | tf_op jit(solution)/shard_map/jit(_roll_static)/slice | solution.py:62
  459.5 8.2 %slice.402 = f32[576,14,255]{0,2,1:T(8,128)} slice(f32[579,14,256]{0,2,1:T(8,128)} %copy-done.10), slice={[0:576], [0:14], [1:256]} | slice | bytes 16450560 | tf_op jit(solution)/shard_map/jit(_roll_static)/slice | solution.py:63
  467.8 5.2 broadcast_add_fusion
  473.0 11.7 %fusion.38 = f32[576,13,256]{0,2,1:T(8,128)} fusion(f32[1,12,256]{0,2,1:T(8,128)S(1)} %copy.98, f32[2,12,256]{0,2,1:T(8,128)S(1)} %copy-done.5, f32[579,1,256]{0,2,1:T(8,128)S(1)} %copy.123, f32[576,12,256]{0,2,1:T(8,128)S(1)} %bitcast.83, f32[576,14,256]{0,2,1:T(8,128)} %broadcast_add_fusion, f32[579,1,256]{0,2,1:T(8,128)S(1)} %copy-done.20), kind=kLoop, calls=%fused_computation.90 | loop fusion | flops 21086208 | bytes 31303680 | tf_op jit(solution)/shard_map/add | solution.py:65
  484.8 10.5 %fusion.19 = f32[576,14,256]{0,2,1:T(8,128)S(1)} fusion(f32[579,14,256]{0,2,1:T(8,128)S(1)} %bitcast.91, f32[576,14,1]{0,2,1:T(1,128)S(1)} %copy-done.36, f32[576,14,255]{0,2,1:T(8,128)} %slice.400, f32[576,14,1]{0,2,1:T(1,128)S(1)} %copy-done.37, f32[576,14,255]{0,2,1:T(8,128)} %slice.402, f32[14,256]{1,0:T(8,128)S(1)} %copy-done.35, f32[576]{0:T(1024)S(1)} %copy-done.32), kind=kLoop, calls=%fused_computation.64 | loop fusion | flops 16515072 | bytes 33046784 | tf_op jit(solution)/shard_map/add | solution.py:61
  495.4 9.5 %fusion.50 = bf16[576,12,256]{0,2,1:T(8,128)(2,1)} fusion(f32[576,12,256]{0,2,1:T(8,128)S(1)} %bitcast.83, f32[576,13,256]{0,2,1:T(8,128)} %fusion.38, f32[576,14,256]{0,2,1:T(8,128)S(1)} %fusion.19, f32[576,14,255]{0,2,1:T(8,128)S(1)} %bitcast.92, f32[576,14,1]{0,2,1:T(1,128)S(1)} %slice.404, f32[12,256]{1,0:T(8,128)S(1)} %copy-done.27), kind=kLoop, calls=%fused_computation.111 | loop fusion | flops 14155776 | bytes 40120320 | tf_op jit(solution)/shard_map/convert_element_type | solution.py:126
  504.9 6.1 copy.126
  511.3 88.4 %all-gather.2.cloned.1.call-done = bf16[1152,3072]{1,0:T(8,128)(2,1)} async-done(((bf16[576,3072]{1,0:T(8,128)(2,1)}), bf16[1152,3072]{1,0:T(8,128)(2,1)}) %all-gather.2.cloned.1.call-update) | async-done | bytes 7077904 | tf_op jit(solution)/shard_map/all_gather | solution.py:129
  599.7 10.5 %fusion.62 = bf16[576,3072]{1,0:T(8,128)(2,1)} fusion(bf16[576,3072]{1,0:T(8,128)(2,1)} %copy.126, bf16[576,1152]{1,0:T(8,128)(2,1)S(1)} %copy-done, bf16[1152,3072]{1,0:T(8,128)(2,1)} %all-gather.2.cloned.1.call-done, f32[3072]{0:T(1024)S(1)} %dynamic_slice.23), kind=kOutput, calls=%fused_computation.139 | convolution fusion | flops 4085710848 | bytes 15495168 | tf_op jit(solution)/shard_map/dot_general | solution.py:132
  610.2 2.1 fusion.63
  (245 shorter events, 76.1 us)
Async XLA Ops:
  7.2 592.5 %copy-start = (bf16[576,1152]{1,0:T(8,128)(2,1)S(1)}, bf16[576,1152]{1,0:T(8,128)(2,1)}, u32[]{:S(2)}) copy-start(bf16[576,1152]{1,0:T(8,128)(2,1)} %param.13) | copy-start | bytes 3981316
  7.2 592.5 %all-gather.2.cloned.1.call-start = ((), (), s32[]{:S(2)}) async-start(), calls=%async_computation | async-start | bytes 10616832 | tf_op jit(solution)/shard_map/all_gather | solution.py:129
  8.8 56.3 %copy-start.23 = (f32[12,256]{1,0:T(8,128)}, f32[12,256]{1,0:T(8,128)S(1)}, u32[]{:S(2)}) copy-start(f32[12,256]{1,0:T(8,128)S(1)} %constant_dynamic-slice_fusion.1) | copy-start | bytes 36868
  65.1 3.9 copy-start.1
  69.0 3.1 copy-start.9
  75.0 19.7 %collective-permute-start.1 = (f32[579,1,256]{2,1,0:T(1,128)}, f32[579,1,256]{2,1,0:T(1,128)}, u32[]{:S(2)}, u32[]{:S(2)}) collective-permute-start(f32[579,1,256]{2,1,0:T(1,128)} %copy.100), channel_id=1, source_target_pairs={{2,0},{4,2},{6,4},{8,6},{10,8},{12,10},{14,12},{16,14},{18,16},{20... | collective-permute-start | bytes 1778696 | tf_op jit(solution)/shard_map/ppermute | solution.py:27
  84.6 22.1 %collective-permute-start = (f32[579,1,256]{2,1,0:T(1,128)}, f32[579,1,256]{2,1,0:T(1,128)}, u32[]{:S(2)}, u32[]{:S(2)}) collective-permute-start(f32[579,1,256]{2,1,0:T(1,128)} %copy.99), channel_id=1, source_target_pairs={{0,2},{2,4},{4,6},{6,8},{8,10},{10,12},{12,14},{14,16},{16,18},{18... | collective-permute-start | bytes 1778696 | tf_op jit(solution)/shard_map/ppermute | solution.py:25
  108.7 7.3 %copy-start.28 = (f32[576]{0:T(1024)S(1)}, f32[576]{0:T(1024)}, u32[]{:S(2)}) copy-start(f32[576]{0:T(1024)} %cosine_multiply_fusion) | copy-start | bytes 6916
  108.7 7.3 %copy-start.38 = (f32[576]{0:T(1024)S(1)}, f32[576]{0:T(1024)}, u32[]{:S(2)}) copy-start(f32[576]{0:T(1024)} %sine_multiply_fusion) | copy-start | bytes 6916
  114.0 6.3 %copy-start.11 = (f32[579,14,256]{0,2,1:T(8,128)}, f32[579,14,256]{0,2,1:T(8,128)S(1)}, u32[]{:S(2)}) copy-start(f32[579,14,256]{0,2,1:T(8,128)S(1)} %fusion.12) | copy-start | bytes 24901636
  120.4 13.8 %slice-start.6 = ((s8[7864320]{0:T(1024)(128)(4,1)}), s8[4194304]{0:T(1024)(128)(4,1)S(1)}, s32[]{:S(2)}) async-start(s8[7864320]{0:T(1024)(128)(4,1)} %bitcast.88), calls=%async_computation.7 | async-start | bytes 8388608
  124.8 9.4 %slice-start.7 = ((s8[7864320]{0:T(1024)(128)(4,1)}), s8[3670016]{0:T(1024)(128)(4,1)S(1)}, s32[]{:S(2)}) async-start(s8[7864320]{0:T(1024)(128)(4,1)} %bitcast.88), calls=%async_computation.8 | async-start | bytes 7340032
  125.9 8.3 %copy-start.2 = (f32[2,12,256]{0,2,1:T(8,128)S(1)}, f32[2,12,256]{0,2,1:T(8,128)}, u32[]{:S(2)}) copy-start(f32[2,12,256]{0,2,1:T(8,128)} %constant_dynamic-slice_fusion) | copy-start | bytes 73732
  125.9 8.3 %copy-start.19 = (f32[579,1,256]{0,2,1:T(8,128)S(1)}, f32[579,1,256]{0,2,1:T(8,128)}, u32[]{:S(2)}) copy-start(f32[579,1,256]{0,2,1:T(8,128)} %copy.101) | copy-start | bytes 1778692
  145.6 15.6 %copy-start.24 = (f32[12,256]{1,0:T(8,128)S(1)}, f32[12,256]{1,0:T(8,128)}, u32[]{:S(2)}) copy-start(f32[12,256]{1,0:T(8,128)} %copy-done.23) | copy-start | bytes 36868
  157.7 3.6 copy-start.14
  175.0 3.1 copy-start.7
  181.0 15.7 %collective-permute-start.3 = (f32[579,1,256]{2,1,0:T(1,128)}, f32[579,1,256]{2,1,0:T(1,128)}, u32[]{:S(2)}, u32[]{:S(2)}) collective-permute-start(f32[579,1,256]{2,1,0:T(1,128)} %copy.107), channel_id=1, source_target_pairs={{2,0},{4,2},{6,4},{8,6},{10,8},{12,10},{14,12},{16,14},{18,16},{20... | collective-permute-start | bytes 1778696 | tf_op jit(solution)/shard_map/ppermute | solution.py:27
  184.5 22.5 %collective-permute-start.2 = (f32[579,1,256]{2,1,0:T(1,128)}, f32[579,1,256]{2,1,0:T(1,128)}, u32[]{:S(2)}, u32[]{:S(2)}) collective-permute-start(f32[579,1,256]{2,1,0:T(1,128)} %copy.106), channel_id=1, source_target_pairs={{0,2},{2,4},{4,6},{6,8},{8,10},{10,12},{12,14},{14,16},{16,18},{18... | collective-permute-start | bytes 1778696 | tf_op jit(solution)/shard_map/ppermute | solution.py:25
  209.0 7.3 %copy-start.29 = (f32[576]{0:T(1024)S(1)}, f32[576]{0:T(1024)}, u32[]{:S(2)}) copy-start(f32[576]{0:T(1024)} %cosine_multiply_fusion) | copy-start | bytes 6916
  214.3 14.7 %copy-start.12 = (f32[579,14,256]{0,2,1:T(8,128)}, f32[579,14,256]{0,2,1:T(8,128)S(1)}, u32[]{:S(2)}) copy-start(f32[579,14,256]{0,2,1:T(8,128)S(1)} %fusion.14) | copy-start | bytes 24901636
  216.9 3.9 copy-start.15
  220.8 20.7 %slice-start.2 = ((s8[7864320]{0:T(1024)(128)(4,1)}), s8[4194304]{0:T(1024)(128)(4,1)S(1)}, s32[]{:S(2)}) async-start(s8[7864320]{0:T(1024)(128)(4,1)} %bitcast.84), calls=%async_computation.3 | async-start | bytes 8388608
  229.0 8.3 %copy-start.39 = (f32[576]{0:T(1024)S(1)}, f32[576]{0:T(1024)}, u32[]{:S(2)}) copy-start(f32[576]{0:T(1024)} %sine_multiply_fusion) | copy-start | bytes 6916
  229.0 12.5 %slice-start.3 = ((s8[7864320]{0:T(1024)(128)(4,1)}), s8[3670016]{0:T(1024)(128)(4,1)S(1)}, s32[]{:S(2)}) async-start(s8[7864320]{0:T(1024)(128)(4,1)} %bitcast.84), calls=%async_computation.4 | async-start | bytes 7340032
  237.3 4.2 copy-start.3
  237.3 4.2 copy-start.21
  253.0 16.9 %copy-start.25 = (f32[12,256]{1,0:T(8,128)S(1)}, f32[12,256]{1,0:T(8,128)}, u32[]{:S(2)}) copy-start(f32[12,256]{1,0:T(8,128)} %copy-done.23) | copy-start | bytes 36868
  283.2 3.1 copy-start.8
  289.3 31.1 %collective-permute-start.5 = (f32[579,1,256]{2,1,0:T(1,128)}, f32[579,1,256]{2,1,0:T(1,128)}, u32[]{:S(2)}, u32[]{:S(2)}) collective-permute-start(f32[579,1,256]{2,1,0:T(1,128)} %copy.114), channel_id=1, source_target_pairs={{2,0},{4,2},{6,4},{8,6},{10,8},{12,10},{14,12},{16,14},{18,16},{20... | collective-permute-start | bytes 1778696 | tf_op jit(solution)/shard_map/ppermute | solution.py:27
  293.2 28.4 %collective-permute-start.4 = (f32[579,1,256]{2,1,0:T(1,128)}, f32[579,1,256]{2,1,0:T(1,128)}, u32[]{:S(2)}, u32[]{:S(2)}) collective-permute-start(f32[579,1,256]{2,1,0:T(1,128)} %copy.113), channel_id=1, source_target_pairs={{0,2},{2,4},{4,6},{6,8},{8,10},{10,12},{12,14},{14,16},{16,18},{18... | collective-permute-start | bytes 1778696 | tf_op jit(solution)/shard_map/ppermute | solution.py:25
  323.7 7.3 %copy-start.30 = (f32[576]{0:T(1024)S(1)}, f32[576]{0:T(1024)}, u32[]{:S(2)}) copy-start(f32[576]{0:T(1024)} %cosine_multiply_fusion) | copy-start | bytes 6916
  329.0 3.6 copy-start.13
  332.5 3.6 copy-start.16
  336.2 21.6 %slice-start.4 = ((s8[7864320]{0:T(1024)(128)(4,1)}), s8[4194304]{0:T(1024)(128)(4,1)S(1)}, s32[]{:S(2)}) async-start(s8[7864320]{0:T(1024)(128)(4,1)} %bitcast.86), calls=%async_computation.5 | async-start | bytes 8388608
  345.3 8.3 %copy-start.40 = (f32[576]{0:T(1024)S(1)}, f32[576]{0:T(1024)}, u32[]{:S(2)}) copy-start(f32[576]{0:T(1024)} %sine_multiply_fusion) | copy-start | bytes 6916
  345.3 12.5 %slice-start.5 = ((s8[7864320]{0:T(1024)(128)(4,1)}), s8[3670016]{0:T(1024)(128)(4,1)S(1)}, s32[]{:S(2)}) async-start(s8[7864320]{0:T(1024)(128)(4,1)} %bitcast.86), calls=%async_computation.6 | async-start | bytes 7340032
  353.6 4.2 copy-start.4
  353.6 4.2 copy-start.22
  369.3 16.9 %copy-start.26 = (f32[12,256]{1,0:T(8,128)S(1)}, f32[12,256]{1,0:T(8,128)}, u32[]{:S(2)}) copy-start(f32[12,256]{1,0:T(8,128)} %copy-done.23) | copy-start | bytes 36868
  399.5 3.1 copy-start.6
  405.5 17.4 %collective-permute-start.7 = (f32[579,1,256]{2,1,0:T(1,128)}, f32[579,1,256]{2,1,0:T(1,128)}, u32[]{:S(2)}, u32[]{:S(2)}) collective-permute-start(f32[579,1,256]{2,1,0:T(1,128)} %copy.121), channel_id=1, source_target_pairs={{2,0},{4,2},{6,4},{8,6},{10,8},{12,10},{14,12},{16,14},{18,16},{20... | collective-permute-start | bytes 1778696 | tf_op jit(solution)/shard_map/ppermute | solution.py:27
  408.6 27.8 %collective-permute-start.6 = (f32[579,1,256]{2,1,0:T(1,128)}, f32[579,1,256]{2,1,0:T(1,128)}, u32[]{:S(2)}, u32[]{:S(2)}) collective-permute-start(f32[579,1,256]{2,1,0:T(1,128)} %copy.120), channel_id=1, source_target_pairs={{0,2},{2,4},{4,6},{6,8},{8,10},{10,12},{12,14},{14,16},{16,18},{18... | collective-permute-start | bytes 1778696 | tf_op jit(solution)/shard_map/ppermute | solution.py:25
  438.4 7.3 %copy-start.31 = (f32[576]{0:T(1024)S(1)}, f32[576]{0:T(1024)}, u32[]{:S(2)}) copy-start(f32[576]{0:T(1024)} %cosine_multiply_fusion) | copy-start | bytes 6916
  443.7 15.2 %copy-start.10 = (f32[579,14,256]{0,2,1:T(8,128)}, f32[579,14,256]{0,2,1:T(8,128)S(1)}, u32[]{:S(2)}) copy-start(f32[579,14,256]{0,2,1:T(8,128)S(1)} %fusion.18) | copy-start | bytes 24901636
  445.7 13.2 %copy-start.34 = (f32[14,256]{1,0:T(8,128)}, f32[14,256]{1,0:T(8,128)S(1)}, u32[]{:S(2)}) copy-start(f32[14,256]{1,0:T(8,128)S(1)} %get-tuple-element.113) | copy-start | bytes 43012
  446.4 3.7 copy-start.17
  450.7 22.3 %slice-start = ((s8[7864320]{0:T(1024)(128)(4,1)}), s8[4194304]{0:T(1024)(128)(4,1)S(1)}, s32[]{:S(2)}) async-start(s8[7864320]{0:T(1024)(128)(4,1)} %bitcast.82), calls=%async_computation.1 | async-start | bytes 8388608
  459.5 8.2 %copy-start.41 = (f32[576]{0:T(1024)S(1)}, f32[576]{0:T(1024)}, u32[]{:S(2)}) copy-start(f32[576]{0:T(1024)} %sine_multiply_fusion) | copy-start | bytes 6916
  459.5 13.5 %slice-start.1 = ((s8[7864320]{0:T(1024)(128)(4,1)}), s8[3670016]{0:T(1024)(128)(4,1)S(1)}, s32[]{:S(2)}) async-start(s8[7864320]{0:T(1024)(128)(4,1)} %bitcast.82), calls=%async_computation.2 | async-start | bytes 7340032
  467.7 5.2 copy-start.5
  467.7 5.2 copy-start.20
  467.7 17.0 %slice-start.8 = ((s8[9175040]{0:T(1024)(128)(4,1)}), s8[4194304]{0:T(1024)(128)(4,1)S(1)}, s32[]{:S(2)}) async-start(s8[9175040]{0:T(1024)(128)(4,1)} %bitcast.90), calls=%async_computation.9 | async-start | bytes 8388608
  473.0 11.8 %slice-start.9 = ((s8[9175040]{0:T(1024)(128)(4,1)}), s8[4194304]{0:T(1024)(128)(4,1)S(1)}, s32[]{:S(2)}) async-start(s8[9175040]{0:T(1024)(128)(4,1)} %bitcast.90), calls=%async_computation.10 | async-start | bytes 8388608
  473.0 11.8 %slice-start.10 = ((s8[9175040]{0:T(1024)(128)(4,1)}), s8[786432]{0:T(1024)(128)(4,1)S(1)}, s32[]{:S(2)}) async-start(s8[9175040]{0:T(1024)(128)(4,1)} %bitcast.90), calls=%async_computation.11 | async-start | bytes 1572864
  473.0 11.8 %copy-start.32 = (f32[576]{0:T(1024)S(1)}, f32[576]{0:T(1024)}, u32[]{:S(2)}) copy-start(f32[576]{0:T(1024)} %cosine_multiply_fusion) | copy-start | bytes 6916
  473.0 11.8 %copy-start.35 = (f32[14,256]{1,0:T(8,128)S(1)}, f32[14,256]{1,0:T(8,128)}, u32[]{:S(2)}) copy-start(f32[14,256]{1,0:T(8,128)} %copy-done.34) | copy-start | bytes 43012
  473.0 11.8 %copy-start.36 = (f32[576,14,1]{0,2,1:T(1,128)S(1)}, f32[576,14,1]{0,2,1:T(1,128)}, u32[]{:S(2)}) copy-start(f32[576,14,1]{0,2,1:T(1,128)} %slice.401) | copy-start | bytes 96772
  473.0 11.8 %copy-start.37 = (f32[576,14,1]{0,2,1:T(1,128)S(1)}, f32[576,14,1]{0,2,1:T(1,128)}, u32[]{:S(2)}) copy-start(f32[576,14,1]{0,2,1:T(1,128)} %slice.403) | copy-start | bytes 96772
  484.8 10.5 %copy-start.27 = (f32[12,256]{1,0:T(8,128)S(1)}, f32[12,256]{1,0:T(8,128)}, u32[]{:S(2)}) copy-start(f32[12,256]{1,0:T(8,128)} %copy-done.23) | copy-start | bytes 36868
  504.9 6.1 copy-start.33
  599.7 10.5 %copy-start.18 = (bf16[1152,3072]{1,0:T(8,128)(2,1)S(1)}, bf16[1152,3072]{1,0:T(8,128)(2,1)}, u32[]{:S(2)}) copy-start(bf16[1152,3072]{1,0:T(8,128)(2,1)} %all-gather.2.cloned.1.call-done) | copy-start | bytes 21233668
Sparse Core Ops, SparseCore 0:
  511.2 88.4 all-gather.1
where the time goes:
time: 627 us; the launch traced here: 619 us
  other arithmetic  227 us (36%)
  waiting for transfers between devices  169 us (27%)
  local copies, waits for them, and re-layouts  151 us (24%)
  starting transfers between devices  28.6 us (5%)
  matrix products  15.6 us (2%)
  between operations  15.1 us (2%)
  blocking collectives  11.3 us (2%)
    all_gather x1, waiting for transfers between devices, per_device(): fragment = lax.all_gather(returned, 'comp', axis=0, tiled=True)  88.4 us
    add x4, other arithmetic, substep(): jnp.maximum(east_speed, 0.0) * energy  54.4 us
    ppermute x4, waiting for transfers between devices, extended(): lax.ppermute(head, axis, [((i + 1) % count, i) for i in range(ends)])  49.3 us
    add x4, other arithmetic, substep(): jnp.maximum(north_speed[:, :-1], 0.0) * energy[:, :-1]  46.1 us
    mul x3, other arithmetic, substep(): return wet_frac[1:-1] * (energy[:, 1:-1] - courant * change)  40.2 us
    slice x8, local copies, waits for them, and re-layouts, substep(): jnp.roll(energy, -1, 2)  35.7 us
    ppermute x4, waiting for transfers between devices, extended(): lax.ppermute(tail, axis, [(i, (i + 1) % count) for i in range(ends)])  31.7 us
    slice x8, local copies, waits for them, and re-layouts, substep(): jnp.roll(east_speed, -1, 2)  29.6 us
  transfers between devices with their start and end apart: 9, of which 8 were waited for; matrix products, arithmetic and copies ran while one was open for 2% of the time, Pallas kernels for 0%

commit v1 on v0

--- a/solution.py
+++ b/solution.py
@@ -1,8 +1,12 @@
+import functools
 import math
 
 import jax
 import jax.numpy as jnp
+import numpy as np
 from jax import lax
+from jax.experimental import pallas as pl
+from jax.experimental.pallas import tpu as pltpu
 from jax.sharding import PartitionSpec as P
 
 NFREQ = 32
@@ -105,7 +109,7 @@
     return jnp.transpose(blocks, (1, 0, 2)).reshape(2, lat_rows, lon_cells)
 
 
-def per_device(spectrum, wet_mask, currents, remap_index, remap_weights, source_matrix):
+def plain_device(spectrum, wet_mask, currents, remap_index, remap_weights, source_matrix):
     wide_count = lax.axis_size("wide")
     wide_index = lax.axis_index("wide")
     comp_index = lax.axis_index("comp")
@@ -138,6 +142,428 @@
     return (updated, drift_part.reshape(2, level_rows, points))
 
 
+CHUNK = 32
+BLOCK = 16
+AHEAD = 4
+TILE = 512
+GROUP = 256
+MESH = pl.DeviceIdType.MESH
+
+
+def speed_table(bin_count, bins_total):
+    index = np.arange(bins_total)
+    group_speed = 0.35 + 0.65 * (NFREQ - 1 - index // NDIR) / (NFREQ - 1)
+    heading = 2.0 * math.pi * (index % NDIR + 0.5) / NDIR
+    both = courant * np.stack([group_speed * np.cos(heading), group_speed * np.sin(heading)])
+    return np.ascontiguousarray(np.broadcast_to(both[:, :, None], (2, bins_total, 128)).astype(np.float32))
+
+
+def drift_table(bins_total, comp_count):
+    index = np.arange(bins_total)
+    frequency = (index // NDIR + 1).astype(np.float32)
+    heading = 2.0 * math.pi * (index % NDIR + 0.5) / NDIR
+    level = np.arange(LEVELS, dtype=np.float32)
+    damping = np.exp(-4.0 * frequency[None, :] * (level[:, None] + 0.5) / (NFREQ * LEVELS))
+    amplitude = damping * (frequency / NFREQ)[None, :] / math.sqrt(NDIR)
+    both = np.stack([amplitude * np.cos(heading), amplitude * np.sin(heading)])
+    both = both.reshape(2, comp_count, LEVELS // comp_count, bins_total)
+    both = np.transpose(both, (1, 0, 2, 3)).reshape(comp_count, -1, bins_total)
+    return both.astype(np.float32).astype(jnp.bfloat16)
+
+
+def wave_kernel(
+    sizes, spec, mask, cur, idx, wgt, src, speed, drift,
+    upd, stk,
+    spec_v, top, bot, prop, other, acc, src_v, parts, speed_v, idx_v, wgt_v,
+    flow, cur_pad, cur_flat, curs, state, coef,
+    load_sem, spec_sem, up_send, down_send, bot_recv, top_recv,
+    cur_send, cur_recv, edge_send, edge_recv, prop_send, prop_recv, out_sem,
+):
+    ns, nw, nc, rows, lon = sizes
+    bins, points = spec.shape
+    depth = SUBSTEPS
+    wide_lanes = depth * lon
+    chunks = bins // CHUNK
+    drift_rows = drift.shape[1]
+    ocean_rows, ocean_cols = cur.shape[1], cur.shape[2]
+    s, w, c = lax.axis_index("strip"), lax.axis_index("wide"), lax.axis_index("comp")
+    place = s * nw + w
+    has_prev = place > 0
+    has_next = place < ns * nw - 1
+    before = jnp.maximum(place - 1, 0)
+    after = jnp.minimum(place + 1, ns * nw - 1)
+    prev_dev = (before // nw, before % nw, c)
+    next_dev = (after // nw, after % nw, c)
+    partner = (s, w, 1 - c)
+
+    def span(k):
+        return pl.ds(pl.multiple_of(k * CHUNK, CHUNK), CHUNK)
+
+    own_rows = pl.ds(pl.multiple_of(c * bins, BLOCK), bins)
+    own_points = pl.ds(pl.multiple_of(w * points, 128), points)
+    loads = [
+        pltpu.make_async_copy(idx.at[:, own_points], idx_v, load_sem.at[0]),
+        pltpu.make_async_copy(wgt.at[:, own_points], wgt_v, load_sem.at[1]),
+        pltpu.make_async_copy(speed.at[:, own_rows, :], speed_v, load_sem.at[2]),
+        pltpu.make_async_copy(src, src_v.at[pl.ds(0, bins), :], load_sem.at[3]),
+        pltpu.make_async_copy(drift.at[c], src_v.at[pl.ds(bins, drift_rows), :], load_sem.at[4]),
+    ]
+
+    def load_chunk(k):
+        return pltpu.make_async_copy(spec.at[span(k), :], spec_v.at[span(k), :], spec_sem.at[k])
+
+    def send_up(k):
+        return pltpu.make_async_remote_copy(
+            src_ref=spec.at[span(k), pl.ds(0, wide_lanes)], dst_ref=bot.at[span(k), :],
+            send_sem=up_send.at[k], recv_sem=bot_recv.at[k], device_id=prev_dev, device_id_type=MESH)
+
+    def send_down(k):
+        return pltpu.make_async_remote_copy(
+            src_ref=spec.at[span(k), pl.ds(points - wide_lanes, wide_lanes)], dst_ref=top.at[span(k), :],
+            send_sem=down_send.at[k], recv_sem=top_recv.at[k], device_id=next_dev, device_id_type=MESH)
+
+    def send_cur(step):
+        return pltpu.make_async_remote_copy(
+            src_ref=cur_flat, dst_ref=curs.at[w], send_sem=cur_send.at[step], recv_sem=cur_recv.at[step],
+            device_id=(s, (w + step + 1) % nw, c), device_id_type=MESH)
+
+    def take_cur(step):
+        return pltpu.make_async_remote_copy(
+            src_ref=cur_flat, dst_ref=curs.at[(w + nw - step - 1) % nw], send_sem=cur_send.at[step],
+            recv_sem=cur_recv.at[step], device_id=(s, (w + step + 1) % nw, c), device_id_type=MESH)
+
+    def send_edge(up):
+        if up:
+            return pltpu.make_async_remote_copy(
+                src_ref=flow.at[:, pl.ds(wide_lanes, wide_lanes)],
+                dst_ref=flow.at[:, pl.ds(wide_lanes + points, wide_lanes)],
+                send_sem=edge_send.at[0], recv_sem=edge_recv.at[0], device_id=prev_dev, device_id_type=MESH)
+        return pltpu.make_async_remote_copy(
+            src_ref=flow.at[:, pl.ds(points, wide_lanes)], dst_ref=flow.at[:, pl.ds(0, wide_lanes)],
+            send_sem=edge_send.at[1], recv_sem=edge_recv.at[1], device_id=next_dev, device_id_type=MESH)
+
+    def send_prop(k):
+        return pltpu.make_async_remote_copy(
+            src_ref=prop.at[span(k), :], dst_ref=other.at[span(k), :],
+            send_sem=prop_send.at[k], recv_sem=prop_recv.at[k], device_id=partner, device_id_type=MESH)
+
+    for copy in loads:
+        copy.start()
+
+    @pl.loop(0, chunks)
+    def _(k):
+        load_chunk(k).start()
+
+    flow[...] = jnp.zeros_like(flow)
+
+    @pl.when(jnp.logical_not(has_prev))
+    def _():
+        top[...] = jnp.zeros_like(top)
+
+    @pl.when(jnp.logical_not(has_next))
+    def _():
+        bot[...] = jnp.zeros_like(bot)
+
+    barrier = pltpu.get_barrier_semaphore()
+    for step in range(1, nw):
+        pl.semaphore_signal(barrier, inc=1, device_id=(s, (w + step) % nw, c), device_id_type=MESH)
+    pl.semaphore_signal(barrier, inc=1, device_id=partner, device_id_type=MESH)
+    cross_prev = jnp.logical_and(has_prev, w == 0)
+    cross_next = jnp.logical_and(has_next, w == nw - 1)
+
+    @pl.when(cross_prev)
+    def _():
+        pl.semaphore_signal(barrier, inc=1, device_id=prev_dev, device_id_type=MESH)
+
+    @pl.when(cross_next)
+    def _():
+        pl.semaphore_signal(barrier, inc=1, device_id=next_dev, device_id_type=MESH)
+
+    cur_pad[...] = jnp.zeros_like(cur_pad)
+    cur_flat[...] = jnp.zeros_like(cur_flat)
+    for comp in range(2):
+        cur_pad[comp, 0:ocean_rows, 0:ocean_cols] = cur[comp]
+        line = cur_pad[comp, 0:1, :]
+        for row in range(1, ocean_rows):
+            line = line + pltpu.roll(cur_pad[comp, row:row + 1, :], row * ocean_cols, 1)
+        cur_flat[comp:comp + 1, :] = line
+    curs[w] = cur_flat[...]
+
+    pl.semaphore_wait(barrier, nw + cross_prev.astype(jnp.int32) + cross_next.astype(jnp.int32))
+
+    for step in range(nw - 1):
+        send_cur(step).start()
+
+    def start_halo(k):
+        @pl.when(has_prev)
+        def _():
+            send_up(k).start()
+
+        @pl.when(has_next)
+        def _():
+            send_down(k).start()
+
+    @pl.loop(0, AHEAD)
+    def _(k):
+        start_halo(k)
+
+    for row in range(rows):
+        lanes = slice(wide_lanes + row * lon, wide_lanes + (row + 1) * lon)
+        flow[2:3, lanes] = mask[pl.ds(w * rows + row, 1), :].astype(jnp.float32)
+    for copy in loads[:2]:
+        copy.wait()
+    for step in range(nw - 1):
+        take_cur(step).wait_recv()
+    total_cols = ocean_cols * nw
+    for piece in range(points // 256):
+        lanes = [slice(piece * 256 + h * 128, piece * 256 + (h + 1) * 128) for h in range(2)]
+        cells = jnp.concatenate([idx_v[:, part] for part in lanes], 0)
+        shares = jnp.concatenate([wgt_v[:, part] for part in lanes], 0)
+        row_of, col_of = cells // total_cols, cells % total_cols
+        tile_of = col_of // ocean_cols
+        spot = row_of * ocean_cols + col_of % ocean_cols
+        for comp in range(2):
+            picked = jnp.zeros(cells.shape, jnp.float32)
+            for tile in range(nw):
+                table = jnp.broadcast_to(curs[tile, comp:comp + 1, :], cells.shape)
+                found = jnp.take_along_axis(table, spot, axis=1, mode="promise_in_bounds")
+                picked = jnp.where(tile_of == tile, found, picked)
+            picked = courant * picked * shares
+            for h in range(2):
+                flow[comp:comp + 1, wide_lanes + piece * 256 + h * 128:wide_lanes + piece * 256 + (h + 1) * 128] = (
+                    jnp.sum(picked[4 * h:4 * h + 4], 0, keepdims=True))
+
+    @pl.when(has_prev)
+    def _():
+        send_edge(True).start()
+
+    @pl.when(has_next)
+    def _():
+        send_edge(False).start()
+
+    for copy in loads[2:]:
+        copy.wait()
+    for half in range(nc):
+        parts[half] = src_v[:, half * bins:(half + 1) * bins]
+
+    @pl.when(has_next)
+    def _():
+        send_edge(True).wait_recv()
+
+    @pl.when(has_prev)
+    def _():
+        send_edge(False).wait_recv()
+
+    ext = rows + 2 * depth
+
+    def at(row):
+        return slice(row * lon, (row + 1) * lon)
+
+    def block(first):
+        here = pl.ds(pl.multiple_of(first, BLOCK), BLOCK)
+        cx = jnp.concatenate([speed_v[0, here, :]] * (lon // 128), 1)
+        cy = jnp.concatenate([speed_v[1, here, :]] * (lon // 128), 1)
+        for row in range(ext):
+            if row < depth:
+                cells = top[here, at(row)]
+            elif row < depth + rows:
+                cells = spec_v[here, at(row - depth)]
+            else:
+                cells = bot[here, at(row - depth - rows)]
+            state[0, :, at(row)] = cells.astype(jnp.float32) * flow[2:3, at(row)]
+
+        def north(row):
+            speed_n = cy + flow[1:2, at(row)]
+            up = jnp.maximum(speed_n, 0.0)
+            return up, up - speed_n
+
+        below, mid = north(0), north(1)
+        for row in range(1, ext - 1):
+            above = north(row + 1)
+            speed_e = cx + flow[0:1, at(row)]
+            east = jnp.maximum(speed_e, 0.0)
+            west = east - speed_e
+            wet = flow[2:3, at(row)]
+            coef[0, :, at(row)] = wet * (1.0 - (east + west) - (mid[0] + mid[1]))
+            coef[1, :, at(row)] = wet * pltpu.roll(east, 1, 1)
+            coef[2, :, at(row)] = wet * pltpu.roll(west, lon - 1, 1)
+            coef[3, :, at(row)] = wet * below[0]
+            coef[4, :, at(row)] = wet * above[1]
+            below, mid = mid, above
+        for repeat in range(depth):
+            now, later = repeat % 2, (repeat + 1) % 2
+            low, mid_e = state[now, :, at(repeat)], state[now, :, at(repeat + 1)]
+            for row in range(repeat + 1, ext - 1 - repeat):
+                high = state[now, :, at(row + 1)]
+                result = (
+                    (coef[0, :, at(row)] * mid_e
+                     + (coef[1, :, at(row)] * pltpu.roll(mid_e, 1, 1)
+                        + coef[2, :, at(row)] * pltpu.roll(mid_e, lon - 1, 1)))
+                    + (coef[3, :, at(row)] * low + coef[4, :, at(row)] * high))
+                if repeat < depth - 1:
+                    state[later, :, at(row)] = result
+                else:
+                    prop[here, at(row - depth)] = result.astype(jnp.bfloat16)
+                low, mid_e = mid_e, high
+
+    @pl.loop(0, chunks)
+    def _(k):
+        load_chunk(k).wait()
+
+        @pl.when(has_next)
+        def _():
+            send_up(k).wait_recv()
+
+        @pl.when(has_prev)
+        def _():
+            send_down(k).wait_recv()
+
+        @pl.when(k + AHEAD < chunks)
+        def _():
+            start_halo(k + AHEAD)
+
+        @pl.loop(0, CHUNK // BLOCK)
+        def _(j):
+            block(k * CHUNK + j * BLOCK)
+
+        send_prop(k).start()
+
+    tiles = points // TILE
+
+    @pl.loop(0, tiles)
+    def _(t):
+        lanes = pl.ds(pl.multiple_of(t * TILE, TILE), TILE)
+        acc[:, lanes] = jnp.dot(parts[c], prop[:, lanes], preferred_element_type=jnp.float32)
+
+    starts = list(range(0, bins, GROUP))
+    for start in starts:
+        size = min(GROUP, bins - start)
+
+        @pl.loop(start // CHUNK, (start + size) // CHUNK)
+        def _(k):
+            send_prop(k).wait_recv()
+
+        @pl.loop(0, tiles)
+        def _(t):
+            lanes = pl.ds(pl.multiple_of(t * TILE, TILE), TILE)
+            total = acc[:, lanes] + jnp.dot(
+                parts[1 - c, :, start:start + size], other[start:start + size, lanes],
+                preferred_element_type=jnp.float32)
+            if start != starts[-1]:
+                acc[:, lanes] = total
+            else:
+                acc[bins:, lanes] = total[bins:]
+                wet = flow[2:3, pl.ds(pl.multiple_of(wide_lanes + t * TILE, 128), TILE)]
+                spec_v[:, lanes] = (
+                    wet * jnp.maximum(prop[:, lanes].astype(jnp.float32) + total[:bins], 0.0)
+                ).astype(jnp.bfloat16)
+                pltpu.make_async_copy(spec_v.at[:, lanes], upd.at[:, lanes], out_sem.at[0, t]).start()
+                pltpu.make_async_copy(
+                    acc.at[pl.ds(bins, drift_rows), lanes], stk.at[:, lanes], out_sem.at[1, t]).start()
+
+    for step in range(nw - 1):
+        send_cur(step).wait_send()
+
+    @pl.when(has_prev)
+    def _():
+        send_edge(True).wait_send()
+
+        @pl.loop(0, chunks)
+        def _(k):
+            send_up(k).wait_send()
+
+    @pl.when(has_next)
+    def _():
+        send_edge(False).wait_send()
+
+        @pl.loop(0, chunks)
+        def _(k):
+            send_down(k).wait_send()
+
+    @pl.loop(0, chunks)
+    def _(k):
+        send_prop(k).wait_send()
+
+    @pl.loop(0, tiles)
+    def _(t):
+        lanes = pl.ds(pl.multiple_of(t * TILE, TILE), TILE)
+        pltpu.make_async_copy(spec_v.at[:, lanes], upd.at[:, lanes], out_sem.at[0, t]).wait()
+        pltpu.make_async_copy(
+            acc.at[pl.ds(bins, drift_rows), lanes], stk.at[:, lanes], out_sem.at[1, t]).wait()
+
+
+def kernel_device(counts, spectrum, wet_mask, currents, remap_index, remap_weights, source_matrix):
+    ns, nw, nc = counts
+    bins, points = spectrum.shape
+    lat_rows, lon = wet_mask.shape
+    rows = lat_rows // nw
+    total = source_matrix.shape[1]
+    drift_rows = 2 * LEVELS // nc
+    chunks = bins // CHUNK
+    tiles = points // TILE
+    edge = SUBSTEPS * lon
+    ext = points + 2 * edge
+    hbm, vmem = pl.BlockSpec(memory_space=pl.ANY), pl.BlockSpec(memory_space=pltpu.VMEM)
+    dma = pltpu.SemaphoreType.DMA
+    bf16, f32 = jnp.bfloat16, jnp.float32
+    updated, stokes = pl.pallas_call(
+        functools.partial(wave_kernel, (ns, nw, nc, rows, lon)),
+        out_shape=(
+            jax.ShapeDtypeStruct((bins, points), bf16),
+            jax.ShapeDtypeStruct((drift_rows, points), f32),
+        ),
+        in_specs=[hbm, vmem, vmem, hbm, hbm, hbm, hbm, hbm],
+        out_specs=(hbm, hbm),
+        scratch_shapes=[
+            pltpu.VMEM((bins, points), bf16),
+            pltpu.VMEM((bins, edge), bf16),
+            pltpu.VMEM((bins, edge), bf16),
+            pltpu.VMEM((bins, points), bf16),
+            pltpu.VMEM((bins, points), bf16),
+            pltpu.VMEM((bins + drift_rows, points), f32),
+            pltpu.VMEM((bins + drift_rows, total), bf16),
+            pltpu.VMEM((nc, bins + drift_rows, bins), bf16),
+            pltpu.VMEM((2, bins, 128), f32),
+            pltpu.VMEM((4, points), jnp.int32),
+            pltpu.VMEM((4, points), f32),
+            pltpu.VMEM((8, ext), f32),
+            pltpu.VMEM((2, 8, 128), f32),
+            pltpu.VMEM((8, 128), f32),
+            pltpu.VMEM((nw, 8, 128), f32),
+            pltpu.VMEM((2, BLOCK, ext), f32),
+            pltpu.VMEM((5, BLOCK, ext), f32),
+            dma((5,)), dma((chunks,)),
+            dma((chunks,)), dma((chunks,)), dma((chunks,)), dma((chunks,)),
+            dma((nw,)), dma((nw,)), dma((2,)), dma((2,)),
+            dma((chunks,)), dma((chunks,)), dma((2, tiles)),
+        ],
+        compiler_params=pltpu.CompilerParams(
+            collective_id=0, has_side_effects=True, vmem_limit_bytes=48 * 1024 * 1024
+        ),
+        name="wave_step",
+    )(
+        spectrum, wet_mask, currents, remap_index, remap_weights, source_matrix,
+        jnp.asarray(speed_table(bins, total)), jnp.asarray(drift_table(total, nc)),
+    )
+    return updated, stokes.reshape(2, LEVELS // nc, points)
+
+
+def per_device(counts, spectrum, wet_mask, currents, remap_index, remap_weights, source_matrix):
+    ns, nw, nc = counts
+    bins, points = spectrum.shape
+    lat_rows, lon = wet_mask.shape
+    rows = lat_rows // nw
+    cells = currents.shape[1] * currents.shape[2]
+    fits = (
+        nc == 2 and nw > 1 and rows >= SUBSTEPS and lon == 256 and points % TILE == 0
+        and bins % CHUNK == 0 and cells <= 128 and currents.shape[1] <= 8
+        and bins // CHUNK >= AHEAD
+    )
+    if fits:
+        return kernel_device(counts, spectrum, wet_mask, currents, remap_index, remap_weights, source_matrix)
+    return plain_device(spectrum, wet_mask, currents, remap_index, remap_weights, source_matrix)
+
+
 def solution(mesh):
     placed = (
         P("comp", ("strip", "wide")),
@@ -147,8 +573,9 @@
         P(None, "strip"),
         P("comp", None),
     )
+    counts = tuple(mesh.shape[axis] for axis in ("strip", "wide", "comp"))
     return jax.shard_map(
-        per_device,
+        functools.partial(per_device, counts),
         mesh=mesh,
         in_specs=placed,
         out_specs=(P("comp", ("strip", "wide")), P(None, "comp", ("strip", "wide"))),

time: 627 us -> 115 us (0.18); the launches traced: 619 us -> 114 us
  other arithmetic: 227 us -> 0 us
  waiting for transfers between devices: 169 us -> 0 us
  local copies, waits for them, and re-layouts: 151 us -> 11.7 us
  Pallas kernels: 0 us -> 102 us
  starting transfers between devices: 28.6 us -> 0 us
  matrix products: 15.6 us -> 0 us
  between operations: 15.1 us -> 0.64 us
  blocking collectives: 11.3 us -> 0 us
    add x16 -> x0, other arithmetic: 120 us -> none  [the longest x4 54.4 us: substep(): jnp.maximum(east_speed, 0.0) * energy]
    pallas_call x0 -> x1, Pallas kernels: none -> 102 us  [kernel_device(): pl.pallas_call(functools.partial(wave_kernel, (ns, nw, nc, rows, lon)), o...]
    slice x36 -> x0, local copies, waits for them, and re-layouts: 91.8 us -> none  [the longest x8 35.7 us: substep(): jnp.roll(energy, -1, 2)]
    all_gather x1 -> x0, waiting for transfers between devices: 88.4 us -> none  [per_device(): fragment = lax.all_gather(returned, 'comp', axis=0, tiled=True)]
    ppermute x8 -> x0, waiting for transfers between devices: 81 us -> none  [the longest x4 49.3 us: extended(): lax.ppermute(head, axis, [((i + 1) % count, i) for i in range(ends)])]
    mul x19 -> x0, other arithmetic: 45.7 us -> none  [the longest x3 40.2 us: substep(): return wet_frac[1:-1] * (energy[:, 1:-1] - courant * change)]
    concatenate x8 -> x0, other arithmetic: 31.9 us -> none  [the longest x4 21.1 us: extended(): jnp.concatenate([lax.ppermute(tail, axis, [(i, (i + 1) % count) for i in...]
    ppermute x8 -> x0, starting transfers between devices: 28.6 us -> none  [the longest x4 15.5 us: extended(): lax.ppermute(head, axis, [((i + 1) % count, i) for i in range(ends)])]
  transfers between devices with their start and end apart: 9 -> 0, of which waited for: 8 -> 0; matrix products, arithmetic and copies ran while one was open for 2% -> 0% of each run, Pallas kernels for 0% -> 0%
where the time goes in v1:
time: 115 us; the launch traced here: 114 us
  Pallas kernels  102 us (89%)
  local copies, waits for them, and re-layouts  11.7 us (10%)
    pallas_call x1, Pallas kernels, kernel_device(): pl.pallas_call(functools.partial(wave_kernel, (ns, nw, nc, rows, lon)), o...  102 us
    unnamed x15, local copies, waits for them, and re-layouts  11.7 us

profile of v1, /device:TPU:1, one launch (start us, length us, event | category | flops | bytes accessed | tf_op | source)
XLA Modules:
  0.0 114.1 jit_solution(6851892424813089374)
XLA Ops:
  0.6 0.8 copy.10.cur
  1.4 0.0 copy-start
  1.4 1.3 %copy-done = bf16[576,1152]{1,0:T(8,128)(2,1)S(1)} copy-done((bf16[576,1152]{1,0:T(8,128)(2,1)S(1)}, bf16[576,1152]{1,0:T(8,128)(2,1)}, u32[]{:S(2)}) %copy-start) | copy-done | bytes 1327128
  2.7 0.0 copy-start.1
  2.7 1.3 %copy-done.1 = f32[2,1152,128]{2,1,0:T(8,128)S(1)} copy-done((f32[2,1152,128]{2,1,0:T(8,128)S(1)}, f32[2,1152,128]{2,1,0:T(8,128)}, u32[]{:S(2)}) %copy-start.1) | copy-done | bytes 1179672
  4.0 0.0 copy-start.2
  4.0 0.9 copy-done.2
  4.9 0.0 copy-start.3
  4.9 0.9 copy-done.3
  5.8 0.0 copy-start.4
  5.8 0.9 copy-done.4
  6.8 0.0 copy-start.5
  6.8 0.8 copy-done.5
  7.6 101.7 %wave_step.1 = (bf16[576,3072]{1,0:T(8,128)(2,1)}, f32[32,3072]{1,0:T(8,128)S(1)}) custom-call(bf16[576,3072]{1,0:T(8,128)(2,1)} %spec.1, s32[48,256]{1,0:T(8,128)S(1)} %copy-done.5, f32[2,8,4]{2,1,0:T(8,128)S(1)} %copy.10.cur, s32[4,12288]{1,0:T(4,128)S(1)} %copy-done.2, f32[4,12288]{1,0:T(4,128)S(1)} %copy-done.3, bf16[576,1152]{1,0:T(8,128)(2,1)S(1)} %copy-done, ...), custom_call_target="tpu_custom_call" | custom-call | tf_op jit(solution)/shard_map/wave_step/pallas_call | solution.py:509
  109.3 4.0 %copy.13 = bf16[576,3072]{1,0:T(8,128)(2,1)} copy(bf16[576,3072]{1,0:T(8,128)(2,1)} %get-tuple-element.8) | data formatting | bytes 7077888
  113.3 0.7 copy.14
Async XLA Ops:
  1.4 1.3 %copy-start = (bf16[576,1152]{1,0:T(8,128)(2,1)S(1)}, bf16[576,1152]{1,0:T(8,128)(2,1)}, u32[]{:S(2)}) copy-start(bf16[576,1152]{1,0:T(8,128)(2,1)} %src.1) | copy-start | bytes 3981316
  2.7 1.3 %copy-start.1 = (f32[2,1152,128]{2,1,0:T(8,128)S(1)}, f32[2,1152,128]{2,1,0:T(8,128)}, u32[]{:S(2)}) copy-start(f32[2,1152,128]{2,1,0:T(8,128)} %constant.4.clone.speed) | copy-start | bytes 3538948
  4.0 0.9 copy-start.2
  4.9 0.9 copy-start.3
  5.8 0.9 copy-start.4
  6.8 0.8 copy-start.5

commit v2 on v1

--- a/solution.py
+++ b/solution.py
@@ -142,9 +142,10 @@
     return (updated, drift_part.reshape(2, level_rows, points))
 
 
-CHUNK = 32
+CHUNK = 16
 BLOCK = 16
-AHEAD = 4
+FIRST = 2
+AHEAD = 8
 TILE = 512
 GROUP = 256
 MESH = pl.DeviceIdType.MESH
@@ -174,18 +175,21 @@
 def wave_kernel(
     sizes, spec, mask, cur, idx, wgt, src, speed, drift,
     upd, stk,
-    spec_v, top, bot, prop, other, acc, src_v, parts, speed_v, idx_v, wgt_v,
+    spec_v, top, bot, prop, other, acc, src_v, parts, speed_v, idx_v, wgt_v, mask_v, cur_v,
     flow, cur_pad, cur_flat, curs, state, coef,
     load_sem, spec_sem, up_send, down_send, bot_recv, top_recv,
-    cur_send, cur_recv, edge_send, edge_recv, prop_send, prop_recv, out_sem,
+    cur_send, cur_recv, edge_send, edge_recv, prop_send, prop_recv, tail_send, tail_recv,
 ):
     ns, nw, nc, rows, lon = sizes
     bins, points = spec.shape
     depth = SUBSTEPS
     wide_lanes = depth * lon
     chunks = bins // CHUNK
+    starts = list(range(0, bins, GROUP))
+    whole = starts[-1] // CHUNK
+    tiles = points // TILE
     drift_rows = drift.shape[1]
-    ocean_rows, ocean_cols = cur.shape[1], cur.shape[2]
+    ocean_cols, ocean_rows = cur.shape[1], cur.shape[2]
     s, w, c = lax.axis_index("strip"), lax.axis_index("wide"), lax.axis_index("comp")
     place = s * nw + w
     has_prev = place > 0
@@ -202,6 +206,8 @@
     own_rows = pl.ds(pl.multiple_of(c * bins, BLOCK), bins)
     own_points = pl.ds(pl.multiple_of(w * points, 128), points)
     loads = [
+        pltpu.make_async_copy(cur, cur_v, load_sem.at[5]),
+        pltpu.make_async_copy(mask, mask_v, load_sem.at[6]),
         pltpu.make_async_copy(idx.at[:, own_points], idx_v, load_sem.at[0]),
         pltpu.make_async_copy(wgt.at[:, own_points], wgt_v, load_sem.at[1]),
         pltpu.make_async_copy(speed.at[:, own_rows, :], speed_v, load_sem.at[2]),
@@ -247,13 +253,14 @@
             src_ref=prop.at[span(k), :], dst_ref=other.at[span(k), :],
             send_sem=prop_send.at[k], recv_sem=prop_recv.at[k], device_id=partner, device_id_type=MESH)
 
-    for copy in loads:
+    def send_tail(t):
+        piece = (pl.ds(starts[-1], bins - starts[-1]), pl.ds(pl.multiple_of(t * TILE, TILE), TILE))
+        return pltpu.make_async_remote_copy(
+            src_ref=prop.at[piece], dst_ref=other.at[piece],
+            send_sem=tail_send.at[t], recv_sem=tail_recv.at[t], device_id=partner, device_id_type=MESH)
+
+    for copy in loads[:4]:
         copy.start()
-
-    @pl.loop(0, chunks)
-    def _(k):
-        load_chunk(k).start()
-
     flow[...] = jnp.zeros_like(flow)
 
     @pl.when(jnp.logical_not(has_prev))
@@ -279,13 +286,20 @@
     def _():
         pl.semaphore_signal(barrier, inc=1, device_id=next_dev, device_id_type=MESH)
 
+    @pl.loop(0, chunks)
+    def _(k):
+        load_chunk(k).start()
+
+    for copy in loads[4:]:
+        copy.start()
     cur_pad[...] = jnp.zeros_like(cur_pad)
+    loads[0].wait()
     cur_flat[...] = jnp.zeros_like(cur_flat)
     for comp in range(2):
-        cur_pad[comp, 0:ocean_rows, 0:ocean_cols] = cur[comp]
+        cur_pad[comp, 0:ocean_cols, 0:ocean_rows] = cur_v[comp]
         line = cur_pad[comp, 0:1, :]
-        for row in range(1, ocean_rows):
-            line = line + pltpu.roll(cur_pad[comp, row:row + 1, :], row * ocean_cols, 1)
+        for col in range(1, ocean_cols):
+            line = line + pltpu.roll(cur_pad[comp, col:col + 1, :], col * ocean_rows, 1)
         cur_flat[comp:comp + 1, :] = line
     curs[w] = cur_flat[...]
 
@@ -303,15 +317,15 @@
         def _():
             send_down(k).start()
 
-    @pl.loop(0, AHEAD)
+    @pl.loop(0, FIRST)
     def _(k):
         start_halo(k)
 
+    for copy in loads[1:4]:
+        copy.wait()
     for row in range(rows):
         lanes = slice(wide_lanes + row * lon, wide_lanes + (row + 1) * lon)
-        flow[2:3, lanes] = mask[pl.ds(w * rows + row, 1), :].astype(jnp.float32)
-    for copy in loads[:2]:
-        copy.wait()
+        flow[2:3, lanes] = mask_v[pl.ds(w * rows + row, 1), :].astype(jnp.float32)
     for step in range(nw - 1):
         take_cur(step).wait_recv()
     total_cols = ocean_cols * nw
@@ -321,7 +335,7 @@
         shares = jnp.concatenate([wgt_v[:, part] for part in lanes], 0)
         row_of, col_of = cells // total_cols, cells % total_cols
         tile_of = col_of // ocean_cols
-        spot = row_of * ocean_cols + col_of % ocean_cols
+        spot = col_of % ocean_cols * ocean_rows + row_of
         for comp in range(2):
             picked = jnp.zeros(cells.shape, jnp.float32)
             for tile in range(nw):
@@ -341,10 +355,11 @@
     def _():
         send_edge(False).start()
 
-    for copy in loads[2:]:
-        copy.wait()
-    for half in range(nc):
-        parts[half] = src_v[:, half * bins:(half + 1) * bins]
+    @pl.loop(FIRST, AHEAD)
+    def _(k):
+        start_halo(k)
+
+    loads[4].wait()
 
     @pl.when(has_next)
     def _():
@@ -422,29 +437,38 @@
         def _():
             start_halo(k + AHEAD)
 
-        @pl.loop(0, CHUNK // BLOCK)
-        def _(j):
-            block(k * CHUNK + j * BLOCK)
-
-        send_prop(k).start()
-
-    tiles = points // TILE
+        block(k * CHUNK)
+
+        @pl.when(k < whole)
+        def _():
+            send_prop(k).start()
+
+    @pl.loop(0, tiles)
+    def _(t):
+        send_tail(t).start()
+
+    for copy in loads[5:]:
+        copy.wait()
+    for half in range(nc):
+        parts[half] = src_v[:, half * bins:(half + 1) * bins]
 
     @pl.loop(0, tiles)
     def _(t):
         lanes = pl.ds(pl.multiple_of(t * TILE, TILE), TILE)
         acc[:, lanes] = jnp.dot(parts[c], prop[:, lanes], preferred_element_type=jnp.float32)
 
-    starts = list(range(0, bins, GROUP))
     for start in starts:
         size = min(GROUP, bins - start)
 
-        @pl.loop(start // CHUNK, (start + size) // CHUNK)
-        def _(k):
-            send_prop(k).wait_recv()
+        if start != starts[-1]:
+            @pl.loop(start // CHUNK, (start + size) // CHUNK)
+            def _(k):
+                send_prop(k).wait_recv()
 
         @pl.loop(0, tiles)
         def _(t):
+            if start == starts[-1]:
+                send_tail(t).wait_recv()
             lanes = pl.ds(pl.multiple_of(t * TILE, TILE), TILE)
             total = acc[:, lanes] + jnp.dot(
                 parts[1 - c, :, start:start + size], other[start:start + size, lanes],
@@ -452,14 +476,11 @@
             if start != starts[-1]:
                 acc[:, lanes] = total
             else:
-                acc[bins:, lanes] = total[bins:]
+                stk[:, lanes] = total[bins:]
                 wet = flow[2:3, pl.ds(pl.multiple_of(wide_lanes + t * TILE, 128), TILE)]
-                spec_v[:, lanes] = (
+                upd[:, lanes] = (
                     wet * jnp.maximum(prop[:, lanes].astype(jnp.float32) + total[:bins], 0.0)
                 ).astype(jnp.bfloat16)
-                pltpu.make_async_copy(spec_v.at[:, lanes], upd.at[:, lanes], out_sem.at[0, t]).start()
-                pltpu.make_async_copy(
-                    acc.at[pl.ds(bins, drift_rows), lanes], stk.at[:, lanes], out_sem.at[1, t]).start()
 
     for step in range(nw - 1):
         send_cur(step).wait_send()
@@ -480,16 +501,13 @@
         def _(k):
             send_down(k).wait_send()
 
-    @pl.loop(0, chunks)
+    @pl.loop(0, whole)
     def _(k):
         send_prop(k).wait_send()
 
     @pl.loop(0, tiles)
     def _(t):
-        lanes = pl.ds(pl.multiple_of(t * TILE, TILE), TILE)
-        pltpu.make_async_copy(spec_v.at[:, lanes], upd.at[:, lanes], out_sem.at[0, t]).wait()
-        pltpu.make_async_copy(
-            acc.at[pl.ds(bins, drift_rows), lanes], stk.at[:, lanes], out_sem.at[1, t]).wait()
+        send_tail(t).wait_send()
 
 
 def kernel_device(counts, spectrum, wet_mask, currents, remap_index, remap_weights, source_matrix):
@@ -503,17 +521,17 @@
     tiles = points // TILE
     edge = SUBSTEPS * lon
     ext = points + 2 * edge
-    hbm, vmem = pl.BlockSpec(memory_space=pl.ANY), pl.BlockSpec(memory_space=pltpu.VMEM)
+    hbm, vmem = pl.BlockSpec(memory_space=pltpu.HBM), pl.BlockSpec(memory_space=pltpu.VMEM)
     dma = pltpu.SemaphoreType.DMA
     bf16, f32 = jnp.bfloat16, jnp.float32
     updated, stokes = pl.pallas_call(
         functools.partial(wave_kernel, (ns, nw, nc, rows, lon)),
         out_shape=(
-            jax.ShapeDtypeStruct((bins, points), bf16),
-            jax.ShapeDtypeStruct((drift_rows, points), f32),
+            pltpu.VMEM((bins, points), bf16),
+            pltpu.VMEM((drift_rows, points), f32),
         ),
-        in_specs=[hbm, vmem, vmem, hbm, hbm, hbm, hbm, hbm],
-        out_specs=(hbm, hbm),
+        in_specs=[hbm] * 8,
+        out_specs=(vmem, vmem),
         scratch_shapes=[
             pltpu.VMEM((bins, points), bf16),
             pltpu.VMEM((bins, edge), bf16),
@@ -526,25 +544,27 @@
             pltpu.VMEM((2, bins, 128), f32),
             pltpu.VMEM((4, points), jnp.int32),
             pltpu.VMEM((4, points), f32),
+            pltpu.VMEM(wet_mask.shape, jnp.int32),
+            pltpu.VMEM((2, currents.shape[2], currents.shape[1]), f32),
             pltpu.VMEM((8, ext), f32),
             pltpu.VMEM((2, 8, 128), f32),
             pltpu.VMEM((8, 128), f32),
             pltpu.VMEM((nw, 8, 128), f32),
             pltpu.VMEM((2, BLOCK, ext), f32),
             pltpu.VMEM((5, BLOCK, ext), f32),
-            dma((5,)), dma((chunks,)),
+            dma((7,)), dma((chunks,)),
             dma((chunks,)), dma((chunks,)), dma((chunks,)), dma((chunks,)),
             dma((nw,)), dma((nw,)), dma((2,)), dma((2,)),
-            dma((chunks,)), dma((chunks,)), dma((2, tiles)),
+            dma((chunks,)), dma((chunks,)), dma((tiles,)), dma((tiles,)),
         ],
         compiler_params=pltpu.CompilerParams(
             collective_id=0, has_side_effects=True, vmem_limit_bytes=48 * 1024 * 1024
         ),
         name="wave_step",
-    )(
-        spectrum, wet_mask, currents, remap_index, remap_weights, source_matrix,
+    )(*(pltpu.with_memory_space_constraint(array, pltpu.HBM) for array in (
+        spectrum, wet_mask, jnp.transpose(currents, (0, 2, 1)), remap_index, remap_weights, source_matrix,
         jnp.asarray(speed_table(bins, total)), jnp.asarray(drift_table(total, nc)),
-    )
+    )))
     return updated, stokes.reshape(2, LEVELS // nc, points)
 
 
@@ -556,7 +576,7 @@
     cells = currents.shape[1] * currents.shape[2]
     fits = (
         nc == 2 and nw > 1 and rows >= SUBSTEPS and lon == 256 and points % TILE == 0
-        and bins % CHUNK == 0 and cells <= 128 and currents.shape[1] <= 8
+        and bins % CHUNK == 0 and cells <= 128 and currents.shape[2] <= 8 and currents.shape[1] <= 128
         and bins // CHUNK >= AHEAD
     )
     if fits:

time: 115 us -> 97.2 us (0.85)
  local copies, waits for them, and re-layouts: 11.7 us -> 2.54 us
  Pallas kernels: 102 us -> 93.9 us
    unnamed x15 -> x2, local copies, waits for them, and re-layouts: 11.7 us -> 2.54 us
    pallas_call x1, Pallas kernels: 102 us -> 93.9 us  [kernel_device(): pl.pallas_call(functools.partial(wave_kernel, (ns, nw, nc, rows, lon)), o...]
where the time goes in v2:
time: 97.2 us; the launch traced here: 97.1 us
  Pallas kernels  93.9 us (97%)
  local copies, waits for them, and re-layouts  2.54 us (3%)
    pallas_call x1, Pallas kernels, kernel_device(): pl.pallas_call(functools.partial(wave_kernel, (ns, nw, nc, rows, lon)), o...  93.9 us
    unnamed x2, local copies, waits for them, and re-layouts  2.54 us

profile of v2, /device:TPU:1, one launch (start us, length us, event | category | flops | bytes accessed | tf_op | source)
XLA Modules:
  0.0 97.1 jit_solution(831536167085645047)
XLA Ops:
  0.6 93.9 %wave_step.1 = (bf16[576,3072]{1,0:T(8,128)(2,1)S(1)}, f32[32,3072]{1,0:T(8,128)S(1)}) custom-call(bf16[576,3072]{1,0:T(8,128)(2,1)} %spec.1, s32[48,256]{1,0:T(8,128)} %mask.1, f32[2,4,8]{2,1,0:T(4,128)} %bitcast.3, s32[4,12288]{1,0:T(4,128)} %idx.1, f32[4,12288]{1,0:T(4,128)} %wgt.1, bf16[576,1152]{1,0:T(8,128)(2,1)} %src.1, ...), custom_call_target="tpu_custom_call" | custom-call | tf_op jit(solution)/shard_map/wave_step/pallas_call | solution.py:527
  94.5 1.8 %copy.12 = bf16[576,3072]{1,0:T(8,128)(2,1)} copy(bf16[576,3072]{1,0:T(8,128)(2,1)S(1)} %get-tuple-element.6) | data formatting | bytes 7077888
  96.3 0.7 copy.13
